TPU v7x, 32 devices: a whole 2x2x4 slice. The times are simulated.
32 devices in a mesh: group: 2 (over x), band: 16 (over z, y, core).
Axes of the slice: x: 2, y: 2, z: 4, core: 2. Of those that a mesh axis runs over, the one named last changes fastest.
Arguments:
- samples: bfloat16 [16384, 2, 4096], P(('group', 'band')), parts along dimension 0, may hold values from -6 to 6
- channel_delay: int32 [8192, 128], P('band'), may hold values from 0 to 15
- merge_rows: int32 [4, 2, 2048], P(None, None, 'band'), may hold values from 0 to 127
- merge_shift: int32 [4, 2048], P(None, 'band'), may hold values from 0 to 63
- destination: int32 [2048], P('band'), may hold values from 0 to 2047, as said below
- widths: int32 [2048], P('band'), may hold values from 1 to 64
Outputs:
- filtered: float32 [4096, 2, 3584], P(('group', 'band')), parts along dimension 0
There are 2 independent parts, one for each index of `group`. A program takes and returns all parts, laid end to end along the dimension named above; an argument that names none is the same for every part. Nothing has to cross between parts.
Inputs may be any that keep to these rules, and one draw needn't show every extreme that they name: destination is a permutation of the trials; the 128 trials of each band go 8 to each owner block of 128 positions, and those of band k land at positions k * 8 to (k + 1) * 8 - 1 of that block.
All inputs are finite; a program needn't handle non-finite values.
Results may differ from a plain program's by a relative error of at most 0.0064.
Values may be sent and summed in bfloat16 or wider, within the bound.
A program may use at most 192 MiB of HBM per device.

v0:
```python
import math

import jax
import jax.numpy as jnp
from jax import lax
from jax.sharding import PartitionSpec as P

MARGIN = 512
DL = 16
DM = 64


half_root = 0.7071067811865476
outer_radix = 16
highest = lax.Precision.HIGHEST


def swapped(value, axis, bit):
    mask = 2**bit
    pairs = [(source, source ^ mask) for source in range(lax.axis_size(axis))]
    return lax.ppermute(value, axis, pairs)


def phase_table(height, breadth, period):
    row_index = lax.broadcasted_iota(jnp.int32, (height, breadth), 0)
    col_index = lax.broadcasted_iota(jnp.int32, (height, breadth), 1)
    angles = (row_index * col_index % period).astype(jnp.float32) * (2.0 * math.pi / period)
    return (jnp.cos(angles), jnp.sin(angles))


def forward_transform(signal):
    inner_size = signal.shape[-1]
    period = outer_radix * inner_size
    cos_outer, sin_outer = phase_table(outer_radix, outer_radix, outer_radix)
    cos_twist, sin_twist = phase_table(outer_radix, inner_size, period)
    cos_inner, sin_inner = phase_table(inner_size, inner_size, inner_size)
    first_real = jnp.einsum("...ab,af->...fb", signal, cos_outer, precision=highest)
    first_imag = -jnp.einsum("...ab,af->...fb", signal, sin_outer, precision=highest)
    twist_real = first_real * cos_twist + first_imag * sin_twist
    twist_imag = first_imag * cos_twist - first_real * sin_twist
    spec_real = jnp.matmul(twist_real, cos_inner, precision=highest) + jnp.matmul(
        twist_imag, sin_inner, precision=highest
    )
    spec_imag = jnp.matmul(twist_imag, cos_inner, precision=highest) - jnp.matmul(
        twist_real, sin_inner, precision=highest
    )
    return (spec_real, spec_imag)


def inverse_transform(spec_real, spec_imag):
    inner_size = spec_real.shape[-1]
    period = outer_radix * inner_size
    cos_outer, sin_outer = phase_table(outer_radix, outer_radix, outer_radix)
    cos_twist, sin_twist = phase_table(outer_radix, inner_size, period)
    cos_inner, sin_inner = phase_table(inner_size, inner_size, inner_size)
    back_real = jnp.matmul(spec_real, cos_inner, precision=highest) - jnp.matmul(
        spec_imag, sin_inner, precision=highest
    )
    back_imag = jnp.matmul(spec_imag, cos_inner, precision=highest) + jnp.matmul(
        spec_real, sin_inner, precision=highest
    )
    turn_real = back_real * cos_twist - back_imag * sin_twist
    turn_imag = back_imag * cos_twist + back_real * sin_twist
    signal = jnp.einsum("...fb,fa->...ab", turn_real, cos_outer, precision=highest) - jnp.einsum(
        "...fb,fa->...ab", turn_imag, sin_outer, precision=highest
    )
    return signal * (1.0 / period)


def shift_rows(high_pick, shift_amounts, out_length):
    extra = (1,) * (high_pick.ndim - 1)
    amounts = shift_amounts.reshape((shift_amounts.shape[0],) + extra)
    result = high_pick
    step_size = 1
    while step_size < DM:
        tail_zeros = jnp.zeros(result.shape[:-1] + (step_size,), result.dtype)
        moved = jnp.concatenate([result[..., step_size:], tail_zeros], axis=result.ndim - 1)
        result = jnp.where(jnp.bitwise_and(amounts, step_size) > 0, moved, result)
        step_size = step_size * 2
    return result[..., :out_length]


def pick_rows(source_rows, picks):
    selector = (
        picks[:, None] == jnp.arange(source_rows.shape[0], dtype=jnp.int32)[None, :]
    ).astype(jnp.bfloat16)
    return jnp.einsum(
        "qr,rsl->qsl", selector, source_rows, preferred_element_type=jnp.float32
    ).astype(jnp.bfloat16)


def merge_step(own_rows, far_rows, low_source, high_source, shift_amounts, upper_bit):
    row_count = own_rows.shape[0]
    length = own_rows.shape[-1]
    stacked = jnp.concatenate([own_rows, far_rows], axis=0)
    low_pick = pick_rows(stacked, low_source + upper_bit * row_count)
    high_pick = pick_rows(stacked, high_source + (1 - upper_bit) * row_count)
    padding = ((0, 0),) * (own_rows.ndim - 1) + ((0, DM),)
    padded = jnp.pad(high_pick, padding)
    moved = shift_rows(padded, shift_amounts, length)
    return ((low_pick.astype(jnp.float32) + moved.astype(jnp.float32)) * half_root).astype(
        jnp.bfloat16
    )


def body(samples, channel_delay, merge_rows, merge_shift, destination, widths):
    channels = samples.shape[0]
    slabs = samples.shape[1]
    length = samples.shape[2]
    row_count = channel_delay.shape[1]
    summed = None
    for delay_value in range(DL):
        select = (channel_delay == delay_value).astype(jnp.bfloat16)
        product = jnp.einsum("cr,csf->rsf", select, samples, preferred_element_type=jnp.float32)
        if delay_value:
            product = jnp.pad(product[:, :, delay_value:], ((0, 0), (0, 0), (0, delay_value)))
        summed = product if summed is None else summed + product
    band_rows = (summed * (1.0 / math.sqrt(channels))).astype(jnp.bfloat16)
    parts_count = lax.axis_size("band")
    level_count = parts_count.bit_length() - 1
    position = lax.axis_index("band")
    inner_size = length // outer_radix
    places = lax.broadcasted_iota(
        jnp.int32, (outer_radix, inner_size), 0
    ) * inner_size + lax.broadcasted_iota(jnp.int32, (outer_radix, inner_size), 1)
    scales = 1.0 / jnp.sqrt(widths.astype(jnp.float32))
    boxcar = jnp.where(
        places[None] < widths[:, None, None], scales[:, None, None], jnp.zeros((), jnp.float32)
    )
    kernel_real, kernel_imag = forward_transform(boxcar)
    kernel_real = kernel_real[:, None]
    kernel_imag = kernel_imag[:, None]
    keep_length = length - MARGIN
    for level_index in range(level_count):
        upper_bit = jnp.bitwise_and(jnp.right_shift(position, level_index), 1)
        far_rows = swapped(band_rows, "band", level_index)
        band_rows = merge_step(
            band_rows,
            far_rows,
            merge_rows[level_index, 0],
            merge_rows[level_index, 1],
            merge_shift[level_index],
            upper_bit,
        )
    share = row_count // parts_count
    owner = destination // row_count
    slot_index = destination % row_count
    placing = owner * share + slot_index - position * share
    placer = (jnp.arange(row_count, dtype=jnp.int32)[:, None] == placing[None, :]).astype(
        jnp.bfloat16
    )
    outgoing = (
        jnp.einsum("pr,rsl->psl", placer, band_rows, preferred_element_type=jnp.float32)
        .astype(jnp.bfloat16)
        .reshape(parts_count, share, slabs, length)
    )
    arrived_block = lax.all_to_all(outgoing, "band", split_axis=0, concat_axis=0, tiled=True)
    sources, share_rows, slab_items, sample_count = arrived_block.shape
    signal = arrived_block.reshape(
        sources * share_rows, slab_items, outer_radix, sample_count // outer_radix
    ).astype(jnp.float32)
    spec_real, spec_imag = forward_transform(signal)
    prod_real = spec_real * kernel_real + spec_imag * kernel_imag
    prod_imag = spec_imag * kernel_real - spec_real * kernel_imag
    series = inverse_transform(prod_real, prod_imag).reshape(
        sources * share_rows, slab_items, sample_count
    )
    result = series[:, :, :keep_length].reshape(sources, share_rows, slab_items, keep_length)
    return result.reshape(row_count, slabs, keep_length)


def solution(mesh):
    return jax.shard_map(
        body,
        mesh=mesh,
        in_specs=(
            P(("group", "band"), None, None),
            P("band", None),
            P(None, None, "band"),
            P(None, "band"),
            P("band"),
            P("band"),
        ),
        out_specs=P(("group", "band"), None, None),
        check_vma=False,
    )
```

profile of v0, /device:TPU:13, one launch (start us, length us, event | category | flops | bytes accessed | tf_op | source)
XLA Modules:
  0.0 526.9 jit_solution(4355678702992629759)
XLA Ops:
  0.0 21.1 %copy.66 = bf16[512,2,4096]{0,2,1:T(8,128)(2,1)} copy(bf16[512,2,4096]{2,1,0:T(2,128)(2,1)} %param.6) | data formatting | bytes 16777216 | tf_op args[0]
  21.1 8.8 %fusion = f32[128,2,4089]{2,0,1:T(8,128)} fusion(bf16[512,2,4096]{0,2,1:T(8,128)(2,1)} %copy.66, s32[512,128]{1,0:T(8,128)S(1)} %copy-done.5), kind=kOutput, calls=%fused_computation | convolution fusion | flops 1071972352 | bytes 12837888 | tf_op jit(solution)/shard_map/cr,csf->rsf/dot_general | solution.py:114
  29.9 5.3 %fusion.10 = f32[128,2,4094]{2,0,1:T(8,128)} fusion(bf16[512,2,4096]{0,2,1:T(8,128)(2,1)S(1)} %copy-done.1, s32[512,128]{1,0:T(8,128)S(1)} %copy-done.5), kind=kOutput, calls=%fused_computation.10 | convolution fusion | flops 1073283072 | bytes 12843008 | tf_op jit(solution)/shard_map/cr,csf->rsf/dot_general | solution.py:114
  35.2 5.3 %fusion.12 = f32[128,2,4095]{2,0,1:T(8,128)} fusion(bf16[512,2,4096]{0,2,1:T(8,128)(2,1)S(1)} %copy-done.1, s32[512,128]{1,0:T(8,128)S(1)} %copy-done.5), kind=kOutput, calls=%fused_computation.12 | convolution fusion | flops 1073545216 | bytes 12844032 | tf_op jit(solution)/shard_map/cr,csf->rsf/dot_general | solution.py:114
  40.4 4.9 fusion.14
  45.3 5.3 %fusion.16 = f32[128,2,4082]{2,0,1:T(8,128)} fusion(bf16[512,2,4096]{0,2,1:T(8,128)(2,1)S(1)} %copy-done.1, s32[512,128]{1,0:T(8,128)S(1)} %copy-done.5), kind=kOutput, calls=%fused_computation.16 | convolution fusion | flops 1070202880 | bytes 12814336 | tf_op jit(solution)/shard_map/cr,csf->rsf/dot_general | solution.py:114
  50.6 4.9 fusion.18
  55.5 5.2 fusion.2
  60.7 4.9 fusion.20
  65.7 4.9 fusion.22
  70.6 5.0 fusion.24
  75.6 5.0 fusion.26
  80.6 4.8 fusion.28
  85.4 5.3 %fusion.4 = f32[128,2,4091]{2,0,1:T(8,128)} fusion(bf16[512,2,4096]{0,2,1:T(8,128)(2,1)S(1)} %copy-done.1, s32[512,128]{1,0:T(8,128)S(1)} %copy-done.5), kind=kOutput, calls=%fused_computation.4 | convolution fusion | flops 1072496640 | bytes 12839936 | tf_op jit(solution)/shard_map/cr,csf->rsf/dot_general | solution.py:114
  90.8 5.3 fusion.6
  96.0 5.6 %fusion.8 = f32[128,2,4093]{2,0,1:T(8,128)} fusion(bf16[512,2,4096]{0,2,1:T(8,128)(2,1)S(1)} %copy-done.1, s32[512,128]{1,0:T(8,128)S(1)} %copy-done.5), kind=kOutput, calls=%fused_computation.8 | convolution fusion | flops 1073020928 | bytes 12841984 | tf_op jit(solution)/shard_map/cr,csf->rsf/dot_general | solution.py:114
  101.7 24.1 %fusion.45 = bf16[128,2,4096]{2,0,1:T(8,128)(2,1)S(1)} fusion(bf16[512,2,4096]{0,2,1:T(8,128)(2,1)} %copy.66, f32[128,2,4081]{2,0,1:T(8,128)} %fusion.14, f32[128,2,4082]{2,0,1:T(8,128)} %fusion.16, f32[128,2,4083]{2,0,1:T(8,128)} %fusion.18, f32[128,2,4084]{2,0,1:T(8,128)} %fusion.20, f32[128,2,4085]{2,0,1:T(8,128)} %fusion.22, ...), kind=kOutput, calls=%fused_computation.46 | convolution fusion | flops 1091633152 | bytes 73539584 | tf_op jit(solution)/shard_map/cr,csf->rsf/dot_general | solution.py:114
  126.6 3.8 collective-permute-done
  130.5 2.3 convolution_convert_fusion.7
  134.3 0.8 slice.254
  135.9 0.8 slice.255
  137.4 0.8 slice.256
  138.9 0.8 slice.257
  140.4 0.8 slice.258
  141.2 3.1 fusion.61
  144.6 46.6 %collective-permute-done.1 = bf16[128,2,4096]{2,0,1:T(8,128)(2,1)S(1)} collective-permute-done((bf16[128,2,4096]{2,0,1:T(8,128)(2,1)S(1)}, bf16[128,2,4096]{2,0,1:T(8,128)(2,1)S(1)}, u32[]{:S(2)}, u32[]{:S(2)}) %collective-permute-start.1) | collective-permute-done | bytes 2097184 | tf_op jit(solution)/shard_map/ppermute | solution.py:21
  192.0 1.0 pad_slice_fusion.2
  193.7 0.8 slice.260
  195.2 0.8 slice.261
  199.8 0.8 slice.264
  200.6 2.2 fusion.57
  203.0 45.8 %collective-permute-done.2 = bf16[128,2,4096]{2,0,1:T(8,128)(2,1)S(1)} collective-permute-done((bf16[128,2,4096]{2,0,1:T(8,128)(2,1)S(1)}, bf16[128,2,4096]{2,0,1:T(8,128)(2,1)S(1)}, u32[]{:S(2)}, u32[]{:S(2)}) %collective-permute-start.2) | collective-permute-done | bytes 2097184 | tf_op jit(solution)/shard_map/ppermute | solution.py:21
  257.1 0.8 slice.270
  257.9 2.4 fusion.53
  260.3 2.4 collective-permute-start.3
  262.7 90.2 %collective-permute-done.3 = bf16[128,2,4096]{2,0,1:T(8,128)(2,1)} collective-permute-done((bf16[128,2,4096]{2,0,1:T(8,128)(2,1)S(1)}, bf16[128,2,4096]{2,0,1:T(8,128)(2,1)}, u32[]{:S(2)}, u32[]{:S(2)}) %collective-permute-start.3) | collective-permute-done | bytes 2097184 | tf_op jit(solution)/shard_map/ppermute | solution.py:21
  352.9 2.3 convolution_convert_fusion.1
  362.8 2.2 slice.276
  365.0 6.0 %fusion.62 = bf16[16,8,2,4096]{3,1,0,2:T(8,128)(2,1)} fusion(bf16[128,2,4096]{2,0,1:T(8,128)(2,1)} %collective-permute-done.3, bf16[128,2,4096]{2,0,1:T(8,128)(2,1)} %copy-done.4, bf16[128,2,4160]{2,0,1:T(8,128)(2,1)S(1)} %pad_select_fusion, bf16[128,2,4128]{2,0,1:T(8,128)(2,1)} %slice.276, pred[128]{0:T(512)(128)(4,1)S(1)} %get-tuple-element.19, ...), kind=kOutput, calls=%fused_computation.72 | convolution fusion | flops 822132736 | bytes 10503680 | tf_op jit(solution)/shard_map/pr,rsl->psl/dot_general | solution.py:153
  371.0 3.1 copy.82
  374.1 7.4 %all-to-all-start = ((bf16[16,8,2,4096]{3,1,2,0:T(8,128)(2,1)}), bf16[16,8,2,4096]{3,1,2,0:T(8,128)(2,1)}, u32[]{:S(2)}, u32[]{:S(2)}) async-start(bf16[16,8,2,4096]{3,1,2,0:T(8,128)(2,1)} %copy.82), calls=%async_computation | async-start | bytes 4194304 | tf_op jit(solution)/shard_map/all_to_all | solution.py:157
  381.8 1.9 fusion.75
  383.7 2.3 add_bitcast_fusion.1
  386.0 3.8 fusion.89
  389.8 4.1 fusion.91
  393.9 3.9 fusion.100
  397.9 5.2 fusion.97
  403.1 25.8 %all-to-all-done = bf16[16,8,2,4096]{3,1,2,0:T(8,128)(2,1)} async-done(((bf16[16,8,2,4096]{3,1,2,0:T(8,128)(2,1)}), bf16[16,8,2,4096]{3,1,2,0:T(8,128)(2,1)}, u32[]{:S(2)}, u32[]{:S(2)}) %all-to-all-start) | async-done | bytes 2097184 | tf_op jit(solution)/shard_map/all_to_all | solution.py:157
  428.9 5.1 copy.83
  434.0 4.7 reshape.456
  438.8 3.6 fusion.216
  442.4 2.6 add_bitcast_fusion
  445.0 6.5 %fusion.69 = f32[128,2,16,256]{3,0,2,1:T(8,128)S(1)} fusion(f32[128,2,16,256]{3,2,1,0:T(8,128)S(1)} %get-tuple-element.8), kind=kOutput, calls=%fused_computation.90 | convolution fusion | flops 3222142976 | bytes 8388608 | tf_op jit(solution)/shard_map/dot_general | solution.py:41
  451.5 6.6 %fusion.67 = f32[128,2,16,256]{3,0,2,1:T(8,128)S(1)} fusion(f32[128,2,16,256]{3,2,1,0:T(8,128)S(1)} %get-tuple-element.8), kind=kOutput, calls=%fused_computation.88 | convolution fusion | flops 3222142976 | bytes 8388608 | tf_op jit(solution)/shard_map/dot_general | solution.py:44
  458.1 7.1 %fusion.83 = f32[128,2,16,256]{3,0,2,1:T(8,128)S(1)} fusion(f32[128,2,16,256]{3,0,2,1:T(8,128)S(1)} %fusion.69, f32[128,2,16,256]{3,2,1,0:T(8,128)S(1)} %get-tuple-element.7), kind=kOutput, calls=%fused_computation.122 | convolution fusion | flops 3223191552 | bytes 12582912 | tf_op jit(solution)/shard_map/dot_general | solution.py:41
  465.2 6.9 %fusion.86 = f32[128,2,16,256]{3,0,2,1:T(8,128)S(1)} fusion(f32[128,2,16,256]{3,0,2,1:T(8,128)S(1)} %fusion.67, f32[128,2,16,256]{3,2,1,0:T(8,128)S(1)} %get-tuple-element.7), kind=kOutput, calls=%fused_computation.123 | convolution fusion | flops 3223191552 | bytes 12582912 | tf_op jit(solution)/shard_map/dot_general | solution.py:44
  472.1 7.1 %fusion.118 = f32[128,2,16,256]{3,0,2,1:T(8,128)} fusion(f32[128,2,16,256]{3,0,2,1:T(8,128)S(1)} %fusion.83, f32[128,2,16,256]{3,0,2,1:T(8,128)S(1)} %fusion.86, f32[128,16,256]{2,0,1:T(8,128)S(1)} %fusion.100, f32[128,16,256]{2,0,1:T(8,128)S(1)} %copy-done), kind=kOutput, calls=%fused_computation.164 | convolution fusion | flops 3225288704 | bytes 16777216 | tf_op jit(solution)/shard_map/dot_general | solution.py:59
  479.2 4.8 fusion.120
  484.0 6.8 %convolution_subtract_fusion = f32[128,2,16,256]{3,0,2,1:T(8,128)} fusion(f32[128,2,16,256]{3,0,2,1:T(8,128)S(1)} %fusion.120, f32[128,2,16,256]{3,0,2,1:T(8,128)S(1)} %fusion.83, f32[128,2,16,256]{3,0,2,1:T(8,128)S(1)} %fusion.86, f32[128,16,256]{2,0,1:T(8,128)S(1)} %fusion.100, f32[128,16,256]{2,0,1:T(8,128)S(1)} %copy-done), kind=kOutput, calls=%fused_computation.125 | convolution fusion | flops 3226337280 | bytes 20971520 | tf_op jit(solution)/shard_map/dot_general | solution.py:56
  490.8 10.9 %multiply_subtract_fusion = (f32[128,2,16,256]{3,0,2,1:T(8,128)}, f32[128,2,16,256]{3,0,2,1:T(8,128)}) fusion(f32[128,2,16,256]{3,0,2,1:T(8,128)} %convolution_subtract_fusion, f32[16,256]{1,0:T(8,128)S(1)} %get-tuple-element.43, f32[16,256]{1,0:T(8,128)S(1)} %get-tuple-element.44, f32[128,2,16,256]{3,0,2,1:T(8,128)} %fusion.118, ...), kind=kOutput, calls=%fused_computation.83 | convolution fusion | flops 3232628736 | bytes 29392896 | tf_op jit(solution)/shard_map/dot_general | solution.py:59
  501.6 8.2 %fusion.63 = f32[16,128,2,256]{3,0,2,1:T(8,128)S(1)} fusion(f32[128,2,16,256]{3,0,2,1:T(8,128)} %get-tuple-element.6), kind=kOutput, calls=%fused_computation.77 | convolution fusion | flops 201330176 | bytes 8388608 | tf_op jit(solution)/shard_map/...fb,fa->...ab/dot_general | solution.py:64
  509.8 6.8 %multiply_bitcast_fusion = f32[128,2,16,256]{3,2,1,0:T(8,128)} fusion(f32[16,128,2,256]{3,0,2,1:T(8,128)S(1)} %fusion.63, f32[128,2,16,256]{3,0,2,1:T(8,128)S(1)} %copy-done.3), kind=kOutput, calls=%fused_computation.81 | convolution fusion | flops 203427328 | bytes 12582912 | tf_op jit(solution)/shard_map/...fb,fa->...ab/dot_general | solution.py:64
  516.6 6.0 %reshape.457 = f32[128,2,4096]{2,1,0:T(2,128)} reshape(f32[128,2,16,256]{3,2,1,0:T(8,128)} %multiply_bitcast_fusion) | data formatting | bytes 8388608 | tf_op jit(solution)/shard_map/reshape | solution.py:165
  522.6 4.1 slice.278
  (66 shorter events, 27.4 us)
Async XLA Ops:
  0.0 21.1 %copy-start.5 = (s32[512,128]{1,0:T(8,128)S(1)}, s32[512,128]{1,0:T(8,128)}, u32[]{:S(2)}) copy-start(s32[512,128]{1,0:T(8,128)} %param.7) | copy-start | bytes 786436
  21.1 8.8 %copy-start.1 = (bf16[512,2,4096]{0,2,1:T(8,128)(2,1)S(1)}, bf16[512,2,4096]{0,2,1:T(8,128)(2,1)}, u32[]{:S(2)}) copy-start(bf16[512,2,4096]{0,2,1:T(8,128)(2,1)} %copy.66) | copy-start | bytes 25165828
  101.6 24.9 %copy-start.6 = (s32[4,128]{1,0:T(4,128)S(1)}, s32[4,128]{1,0:T(4,128)}, u32[]{:S(2)}) copy-start(s32[4,128]{1,0:T(4,128)} %param.9) | copy-start | bytes 6148
  101.6 24.9 %copy-start.7 = (s32[4,2,128]{2,1,0:T(2,128)S(1)}, s32[4,2,128]{2,1,0:T(2,128)}, u32[]{:S(2)}) copy-start(s32[4,2,128]{2,1,0:T(2,128)} %param.8) | copy-start | bytes 12292
  125.8 4.7 collective-permute-start
  144.4 46.9 %collective-permute-start.1 = (bf16[128,2,4096]{2,0,1:T(8,128)(2,1)S(1)}, bf16[128,2,4096]{2,0,1:T(8,128)(2,1)S(1)}, u32[]{:S(2)}, u32[]{:S(2)}) collective-permute-start(bf16[128,2,4096]{2,0,1:T(8,128)(2,1)S(1)} %fusion.61), channel_id=1, source_target_pairs={{0,2},{1,3},{2,0},{3,1},{4,6},{5,7},{6,4},{7,5},{8,10},{9,11},{10,... | collective-permute-start | bytes 6291464 | tf_op jit(solution)/shard_map/ppermute | solution.py:21
  202.8 46.0 %collective-permute-start.2 = (bf16[128,2,4096]{2,0,1:T(8,128)(2,1)S(1)}, bf16[128,2,4096]{2,0,1:T(8,128)(2,1)S(1)}, u32[]{:S(2)}, u32[]{:S(2)}) collective-permute-start(bf16[128,2,4096]{2,0,1:T(8,128)(2,1)S(1)} %fusion.57), channel_id=1, source_target_pairs={{0,4},{1,5},{2,6},{3,7},{4,0},{5,1},{6,2},{7,3},{8,12},{9,13},{10,... | collective-permute-start | bytes 6291464 | tf_op jit(solution)/shard_map/ppermute | solution.py:21
  257.9 4.8 copy-start.9
  260.3 94.9 %copy-start.4 = (bf16[128,2,4096]{2,0,1:T(8,128)(2,1)}, bf16[128,2,4096]{2,0,1:T(8,128)(2,1)S(1)}, u32[]{:S(2)}) copy-start(bf16[128,2,4096]{2,0,1:T(8,128)(2,1)S(1)} %fusion.53) | copy-start | bytes 6291460
  260.3 92.6 %collective-permute-start.3 = (bf16[128,2,4096]{2,0,1:T(8,128)(2,1)S(1)}, bf16[128,2,4096]{2,0,1:T(8,128)(2,1)}, u32[]{:S(2)}, u32[]{:S(2)}) collective-permute-start(bf16[128,2,4096]{2,0,1:T(8,128)(2,1)S(1)} %fusion.53), channel_id=1, source_target_pairs={{0,8},{1,9},{2,10},{3,11},{4,12},{5,13},{6,14},{7,15},{8,0},{9,1},... | collective-permute-start | bytes 6291464 | tf_op jit(solution)/shard_map/ppermute | solution.py:21
  371.0 10.7 %copy-start.8 = (s32[128]{0:T(128)S(1)}, s32[128]{0:T(128)}, u32[]{:S(2)}) copy-start(s32[128]{0:T(128)} %param.11) | copy-start | bytes 1540
  374.1 54.8 %all-to-all-start = ((bf16[16,8,2,4096]{3,1,2,0:T(8,128)(2,1)}), bf16[16,8,2,4096]{3,1,2,0:T(8,128)(2,1)}, u32[]{:S(2)}, u32[]{:S(2)}) async-start(bf16[16,8,2,4096]{3,1,2,0:T(8,128)(2,1)} %copy.82), calls=%async_computation | async-start | bytes 4194304 | tf_op jit(solution)/shard_map/all_to_all | solution.py:157
  438.8 3.6 copy-start.2
  465.2 6.9 %copy-start = (f32[128,16,256]{2,0,1:T(8,128)S(1)}, f32[128,16,256]{2,0,1:T(8,128)}, u32[]{:S(2)}) copy-start(f32[128,16,256]{2,0,1:T(8,128)} %fusion.97) | copy-start | bytes 6291460
  501.6 8.2 %copy-start.3 = (f32[128,2,16,256]{3,0,2,1:T(8,128)S(1)}, f32[128,2,16,256]{3,0,2,1:T(8,128)}, u32[]{:S(2)}) copy-start(f32[128,2,16,256]{3,0,2,1:T(8,128)} %get-tuple-element.5) | copy-start | bytes 12582916
where the time goes:
time: 537 us; the launch traced here: 527 us
  matrix products  224 us (42%)
  waiting for transfers between devices  212 us (39%)
  local copies, waits for them, and re-layouts  65.3 us (12%)
  other arithmetic  14 us (3%)
  starting transfers between devices  11.1 us (2%)
    ppermute x4, waiting for transfers between devices, swapped(): return lax.ppermute(value, axis, pairs)  186 us
    dot_general x16, matrix products, body(): jnp.einsum('cr,csf->rsf', select, samples, preferred_element_type=jnp.flo...  105 us
    all_to_all x1, waiting for transfers between devices, body(): lax.all_to_all(outgoing, 'band', split_axis=0, concat_axis=0, tiled=True)  25.8 us
    unnamed x21, local copies, waits for them, and re-layouts  21.1 us
    slice x24, local copies, waits for them, and re-layouts, shift_rows(): result[..., step_size:]  21.1 us
    dot_general x7, matrix products, pick_rows(): jnp.einsum('qr,rsl->qsl', selector, source_rows, preferred_element_type=j...  13.8 us
    select_n x20, other arithmetic, shift_rows(): result = jnp.where(jnp.bitwise_and(amounts, step_size) > 0, moved, result)  13.8 us
    dot_general x2, matrix products, forward_transform(): jnp.matmul(twist_real, cos_inner, precision=highest)  12.3 us
  transfers between devices with their start and end apart: 5, of which 5 were waited for; matrix products, arithmetic and copies ran while one was open for 4% of the time, Pallas kernels for 0%

commit v1 on v0

v1 whole, which is shorter than its diff:
```python
import functools
import math

import jax
import jax.numpy as jnp
from jax import lax
from jax.experimental import pallas as pl
from jax.experimental.pallas import tpu as pltpu
from jax.sharding import PartitionSpec as P

MARGIN = 512
DL = 16
DM = 64
LANES = 128
SUBLANES = 8
GROUP = 16
half_root = 0.7071067811865476
f32 = jnp.float32
bf16 = jnp.bfloat16
VMEM_BYTES = 58 * 2**20


def level0_kernel(chunks, chunk, halo, delay_ref, x_ref, next_ref, out_ref, sel_ref):
    slab = pl.program_id(0)
    piece = pl.program_id(1)
    rows = delay_ref.shape[0]
    channels = delay_ref.shape[1]

    @pl.when((slab == 0) & (piece == 0))
    def _():
        for d in range(DL):
            sel_ref[d * rows : (d + 1) * rows, :] = jnp.where(
                delay_ref[...] == d, 1.0, 0.0
            ).astype(bf16)

    alive = jnp.where(piece + 1 < chunks, 1.0, 0.0).astype(bf16)
    x = jnp.concatenate([x_ref[0], next_ref[0] * alive], axis=1)
    total = jnp.zeros((rows, chunk), f32)
    per = 4
    for first in range(0, DL, per):
        y = jnp.dot(
            sel_ref[first * rows : (first + per) * rows, :], x, preferred_element_type=f32
        )
        for d in range(first, first + per):
            part = y[(d - first) * rows : (d - first + 1) * rows, :]
            total = total + part[:, d : d + chunk]
    value = (total * (1.0 / math.sqrt(channels))).astype(bf16)
    here = slab * chunks + piece
    out_ref[pl.ds(here, 1), :, 0:chunk] = value[None]
    reach = -(-halo // chunk)
    for back in range(1, reach + 1):
        stop = min((back + 1) * chunk, chunk + halo)
        width = stop - back * chunk

        @pl.when(piece >= back)
        def _():
            out_ref[pl.ds(here - back, 1), :, back * chunk : stop] = value[None, :, :width]

        @pl.when(piece + back >= chunks)
        def _():
            out_ref[pl.ds(here, 1), :, back * chunk : stop] = jnp.zeros((1, rows, width), bf16)


def level0(samples, channel_delay, parts, halo):
    slabs, channels, length = samples.shape
    rows = channel_delay.shape[1]
    chunks = parts // slabs
    chunk = length // chunks
    tiles = chunk // LANES
    last = length // LANES - 1
    return pl.pallas_call(
        functools.partial(level0_kernel, chunks, chunk, halo),
        grid=(slabs, chunks),
        in_specs=[
            pl.BlockSpec((rows, channels), lambda s, c: (0, 0)),
            pl.BlockSpec((1, channels, chunk), lambda s, c: (s, 0, c)),
            pl.BlockSpec(
                (1, channels, LANES), lambda s, c: (s, 0, jnp.minimum((c + 1) * tiles, last))
            ),
        ],
        out_specs=pl.BlockSpec((parts, rows, chunk + halo), lambda s, c: (0, 0, 0)),
        out_shape=jax.ShapeDtypeStruct((parts, rows, chunk + halo), bf16),
        scratch_shapes=[pltpu.VMEM((DL * rows, channels), bf16)],
        compiler_params=pltpu.CompilerParams(vmem_limit_bytes=VMEM_BYTES),
        name="level0",
    )(channel_delay.T, samples, samples)


def tree_kernel(levels, keep, table_ref, dest_ref, x_ref, out_ref, a_ref, b_ref, o_ref):
    trials, extent = x_ref.shape
    rows = out_ref.shape[1]

    def stage(g, carry):
        x = x_ref[pl.ds(pl.multiple_of(g * GROUP, GROUP), GROUP), :].astype(f32)
        for j in range(SUBLANES):
            if j * LANES < extent:
                piece = x[:, j * LANES : (j + 1) * LANES]
            else:
                piece = jnp.zeros((GROUP, LANES), f32)
            a_ref[pl.ds(g * GROUP * SUBLANES + j, GROUP, stride=SUBLANES), :] = piece
        return carry

    lax.fori_loop(0, trials // GROUP, stage, 0)
    lane = lax.broadcasted_iota(jnp.int32, (SUBLANES, LANES), 1)
    for level in range(levels):
        src, dst = (a_ref, b_ref) if level % 2 == 0 else (b_ref, a_ref)

        def merge(g, carry):
            values = []
            for i in range(GROUP):
                word = table_ref[level, g * GROUP + i]
                low = jnp.bitwise_and(word, 4095)
                high = jnp.bitwise_and(jnp.right_shift(word, 12), 4095)
                shift = jnp.right_shift(word, 24)
                v_low = src[pl.ds(pl.multiple_of(low * SUBLANES, SUBLANES), SUBLANES), :]
                v_high = src[pl.ds(pl.multiple_of(high * SUBLANES, SUBLANES), SUBLANES), :]
                turned = pltpu.roll(v_high, jnp.bitwise_and(LANES - shift, LANES - 1), 1)
                after = pltpu.roll(turned, SUBLANES - 1, 0)
                moved = jnp.where(lane < LANES - shift, turned, after)
                values.append(((v_low + moved) * half_root).astype(bf16).astype(f32))
            for i in range(GROUP):
                q = g * GROUP + i
                if level + 1 < levels:
                    dst[pl.ds(pl.multiple_of(q * SUBLANES, SUBLANES), SUBLANES), :] = values[i]
                else:
                    o_ref[pl.ds(dest_ref[q], keep, stride=rows), :] = values[i][:keep]
            return carry

        lax.fori_loop(0, trials // GROUP, merge, 0)

    def pack(g, carry):
        out_ref[g] = o_ref[pl.ds(pl.multiple_of(g * rows, rows), rows), :].astype(bf16)
        return carry

    lax.fori_loop(0, out_ref.shape[0], pack, 0)


def tree(table, places, arrived, keep, rows):
    levels = table.shape[0]
    trials = arrived.shape[0]
    blocks = trials // rows * keep
    whole = pl.BlockSpec(memory_space=pltpu.VMEM)
    scalars = pl.BlockSpec(memory_space=pltpu.SMEM)
    return pl.pallas_call(
        functools.partial(tree_kernel, levels, keep),
        in_specs=[scalars, scalars, whole],
        out_specs=whole,
        out_shape=jax.ShapeDtypeStruct((blocks, rows, LANES), bf16),
        scratch_shapes=[
            pltpu.VMEM((trials * SUBLANES, LANES), f32),
            pltpu.VMEM((trials * SUBLANES, LANES), f32),
            pltpu.VMEM((blocks * rows, LANES), f32),
        ],
        compiler_params=pltpu.CompilerParams(vmem_limit_bytes=VMEM_BYTES),
        name="tree",
    )(table, places, arrived)


PITCH = 40


def boxcar_kernel(slabs, valid, widths_ref, scales_ref, x_ref, out_ref, p_ref, t_ref):
    blocks, rows, _ = x_ref.shape
    per_slab = blocks // slabs
    row = lax.broadcasted_iota(jnp.int32, (LANES, 2 * LANES), 0)
    col = lax.broadcasted_iota(jnp.int32, (LANES, 2 * LANES), 1)
    sums = jnp.where(row < col, 1.0, 0.0).astype(bf16)

    def prefix(i, carry):
        for s in range(slabs):
            y = jnp.dot(x_ref[s * per_slab + i], sums, preferred_element_type=f32)
            p_ref[pl.ds(s * rows * PITCH + i, rows, stride=PITCH), :] = y[:, :LANES]
            t_ref[pl.ds(s * rows * PITCH + i, rows, stride=PITCH), :] = y[:, LANES:]
        return carry

    lax.fori_loop(0, valid + 1, prefix, 0)
    lane = lax.broadcasted_iota(jnp.int32, (SUBLANES, LANES), 1)

    def window(g, carry):
        for i in range(2):
            p = g * 2 + i
            width = widths_ref[p]
            scale = scales_ref[p]
            amount = LANES - width
            for s in range(slabs):
                base = pl.multiple_of((s * rows + p) * PITCH, SUBLANES)
                for b in range(0, valid, SUBLANES):
                    here = p_ref[pl.ds(base + b, SUBLANES), :]
                    after = p_ref[pl.ds(base + b + 1, SUBLANES), :]
                    whole = t_ref[pl.ds(base + b, SUBLANES), :]
                    end = jnp.where(
                        lane < amount,
                        pltpu.roll(here, amount, 1),
                        pltpu.roll(after, amount, 1) + whole,
                    )
                    value = (end - here) * scale
                    count = min(SUBLANES, valid - b)
                    out_ref[pl.ds(p * (valid * slabs) + b * slabs + s, count, stride=slabs), :] = value[:count]
        return carry

    lax.fori_loop(0, rows // 2, window, 0)


def boxcar(widths, arrived, slabs, valid):
    rows = arrived.shape[1]
    whole = pl.BlockSpec(memory_space=pltpu.VMEM)
    scalars = pl.BlockSpec(memory_space=pltpu.SMEM)
    return pl.pallas_call(
        functools.partial(boxcar_kernel, slabs, valid),
        in_specs=[scalars, scalars, whole],
        out_specs=whole,
        out_shape=jax.ShapeDtypeStruct((rows * valid * slabs, LANES), f32),
        scratch_shapes=[
            pltpu.VMEM((slabs * rows * PITCH, LANES), f32),
            pltpu.VMEM((slabs * rows * PITCH, LANES), f32),
        ],
        compiler_params=pltpu.CompilerParams(vmem_limit_bytes=VMEM_BYTES),
        name="boxcar",
    )(widths, 1.0 / jnp.sqrt(widths.astype(f32)), arrived)


def body(samples, channel_delay, merge_rows, merge_shift, destination, widths):
    slabs, length = samples.shape[1], samples.shape[2]
    rows = channel_delay.shape[1]
    parts = lax.axis_size("band")
    levels = merge_shift.shape[0]
    position = lax.axis_index("band")
    chunk = slabs * length // parts
    keep = chunk // LANES
    halo = -(-levels * (DM - 1) // LANES) * LANES

    bits = (2 ** jnp.arange(levels, dtype=jnp.int32))[:, None]
    low = (position & ~bits) * rows + merge_rows[:, 0]
    high = (position | bits) * rows + merge_rows[:, 1]
    owner, slot = destination // rows, destination % rows
    place = owner * (keep * rows) + slot
    tables = jnp.concatenate([low, high, merge_shift, place[None]], axis=0)
    tables = lax.all_gather(tables, "band", axis=1, tiled=True)
    table = (
        tables[:levels]
        + tables[levels : 2 * levels] * 4096
        + tables[2 * levels : 3 * levels] * (4096 * 4096)
    )
    places = tables[3 * levels]

    outgoing = level0(jnp.transpose(samples, (1, 0, 2)), channel_delay, parts, halo)
    arrived = lax.all_to_all(outgoing, "band", split_axis=0, concat_axis=0, tiled=True)
    merged = tree(table, places, arrived.reshape(parts * rows, chunk + halo), keep, rows)
    grouped = lax.all_to_all(merged, "band", split_axis=0, concat_axis=0, tiled=True)
    valid = (length - MARGIN) // LANES
    result = boxcar(widths, grouped, slabs, valid)
    result = result.reshape(rows, valid, slabs, LANES).transpose(0, 2, 1, 3)
    return result.reshape(rows, slabs, valid * LANES)


def solution(mesh):
    return jax.shard_map(
        body,
        mesh=mesh,
        in_specs=(
            P(("group", "band"), None, None),
            P("band", None),
            P(None, None, "band"),
            P(None, "band"),
            P("band"),
            P("band"),
        ),
        out_specs=P(("group", "band"), None, None),
        check_vma=False,
    )
```

time: 537 us -> 297 us (0.55); the launches traced: 527 us -> 296 us
  matrix products: 224 us -> 0 us
  waiting for transfers between devices: 212 us -> 46.9 us
  Pallas kernels: 0 us -> 126 us
  blocking collectives: 0 us -> 79.5 us
  local copies, waits for them, and re-layouts: 65.3 us -> 30.5 us
  other arithmetic: 14 us -> 1.29 us
    dot_general x42 -> x0, matrix products: 224 us -> none  [the longest x16 105 us: body(): jnp.einsum('cr,csf->rsf', select, samples, preferred_element_type=jnp.flo...]
    ppermute x4 -> x0, waiting for transfers between devices: 186 us -> none  [swapped(): return lax.ppermute(value, axis, pairs)]
    pallas_call x0 -> x3, Pallas kernels: none -> 126 us  [the longest x1 74.1 us: tree(): pl.pallas_call(functools.partial(tree_kernel, levels, keep), in_specs=[sc...]
    all_gather x0 -> x1, blocking collectives: none -> 79.5 us  [body(): tables = lax.all_gather(tables, 'band', axis=1, tiled=True)]
    all_to_all x0 -> x1, waiting for transfers between devices: none -> 46.9 us  [body(): lax.all_to_all(merged, 'band', split_axis=0, concat_axis=0, tiled=True)]
    all_to_all x1, waiting for transfers between devices: 25.8 us -> 0.01 us  [body(): lax.all_to_all(outgoing, 'band', split_axis=0, concat_axis=0, tiled=True)]
    slice x25 -> x2, local copies, waits for them, and re-layouts: 25.2 us -> 0.61 us  [the longest x1 0.6 us: body(): places = tables[3 * levels]]
    select_n x20 -> x0, other arithmetic: 13.8 us -> none  [shift_rows(): result = jnp.where(jnp.bitwise_and(amounts, step_size) > 0, moved, result)]
  transfers between devices with their start and end apart: 5 -> 2, of which waited for: 5 -> 1; matrix products, arithmetic and copies ran while one was open for 4% -> 1% of each run, Pallas kernels for 0% -> 0%
where the time goes in v1:
time: 297 us; the launch traced here: 296 us
  Pallas kernels  126 us (42%)
  blocking collectives  79.5 us (27%)
  waiting for transfers between devices  46.9 us (16%)
  local copies, waits for them, and re-layouts  30.5 us (10%)
  starting transfers between devices  11.8 us (4%)
    all_gather x1, blocking collectives, body(): tables = lax.all_gather(tables, 'band', axis=1, tiled=True)  79.5 us
    pallas_call x1, Pallas kernels, tree(): pl.pallas_call(functools.partial(tree_kernel, levels, keep), in_specs=[sc...  74.1 us
    all_to_all x1, waiting for transfers between devices, body(): lax.all_to_all(merged, 'band', split_axis=0, concat_axis=0, tiled=True)  46.9 us
    pallas_call x1, Pallas kernels, level0(): pl.pallas_call(functools.partial(level0_kernel, chunks, chunk, halo), gri...  36.1 us
    unnamed x16, local copies, waits for them, and re-layouts  16.6 us
    pallas_call x1, Pallas kernels, boxcar(): pl.pallas_call(functools.partial(boxcar_kernel, slabs, valid), in_specs=[...  15.8 us
    reshape x1, local copies, waits for them, and re-layouts, body(): result = result.reshape(rows, valid, slabs, LANES).transpose(0, 2, 1, 3)  6.71 us
    all_to_all x1, starting transfers between devices, body(): lax.all_to_all(outgoing, 'band', split_axis=0, concat_axis=0, tiled=True)  6.7 us
  transfers between devices with their start and end apart: 2, of which 1 were waited for; matrix products, arithmetic and copies ran while one was open for 1% of the time, Pallas kernels for 0%

profile of v1, /device:TPU:13, one launch (start us, length us, event | category | flops | bytes accessed | tf_op | source)
XLA Modules:
  0.0 296.0 jit_solution(13002720494326753101)
XLA Ops:
  0.0 0.0 copy-start.2
  0.0 12.7 %copy.21 = bf16[512,2,4096]{2,0,1:T(8,128)(2,1)} copy(bf16[512,2,4096]{2,1,0:T(2,128)(2,1)} %param.6) | data formatting | bytes 16777216 | tf_op args[0]
  12.7 0.0 copy-done.2
  12.7 0.9 copy.14
  13.6 36.1 %level0.1 = bf16[16,128,768]{2,1,0:T(8,128)(2,1)} custom-call(s32[128,512]{1,0:T(8,128)} %bitcast.23, bf16[2,512,4096]{2,1,0:T(8,128)(2,1)} %bitcast.18, bf16[2,512,4096]{2,1,0:T(8,128)(2,1)} %bitcast.19), custom_call_target="tpu_custom_call" | custom-call | tf_op jit(solution)/shard_map/level0/pallas_call | solution.py:71
  49.6 0.0 copy-start.6
  49.6 0.0 copy-start.3
  49.6 0.0 copy-start.4
  49.6 6.7 %all-to-all-start = ((bf16[16,128,768]{2,1,0:T(8,128)(2,1)}), bf16[16,128,768]{2,1,0:T(8,128)(2,1)S(1)}, u32[]{:S(2)}, u32[]{:S(2)}) async-start(bf16[16,128,768]{2,1,0:T(8,128)(2,1)} %level0.1), calls=%async_computation | async-start | bytes 6291456 | tf_op jit(solution)/shard_map/all_to_all | solution.py:247
  56.3 0.0 copy-done.6
  56.4 0.0 copy-done.3
  56.4 0.1 broadcast_add_fusion
  56.5 0.1 broadcast_add_fusion.1
  56.5 0.0 copy-done.4
  56.5 79.5 %all_gather.3 = s32[13,2048]{1,0:T(8,128)S(1)} all-gather(s32[13,128]{1,0:T(8,128)S(1)} %pad_add_fusion), channel_id=1, replica_groups=mesh['group'=2,'band'=16] {'band'}, dimensions={1}, use_global_device_ids=true | all-gather | bytes 113152 | tf_op jit(solution)/shard_map/all_gather | solution.py:238
  136.0 0.6 slice.27
  136.6 0.6 fusion.table_ref
  137.2 0.0 all-to-all-done
  137.3 0.0 copy-start
  137.3 1.7 copy-done
  138.9 0.0 copy-start.5
  138.9 74.1 %tree.1 = bf16[64,128,128]{2,1,0:T(8,128)(2,1)} custom-call(s32[4,2048]{1,0:T(4,128)} %fusion.table_ref, s32[2048]{0:T(1024)} %bitcast.24, bf16[2048,768]{1,0:T(8,128)(2,1)} %bitcast.22), custom_call_target="tpu_custom_call" | custom-call | tf_op jit(solution)/shard_map/tree/pallas_call | solution.py:144
  213.0 5.1 %all-to-all-start.1 = ((bf16[64,128,128]{2,1,0:T(8,128)(2,1)}), bf16[64,128,128]{2,1,0:T(8,128)(2,1)S(1)}, u32[]{:S(2)}, u32[]{:S(2)}) async-start(bf16[64,128,128]{2,1,0:T(8,128)(2,1)} %tree.1), calls=%async_computation.1 | async-start | bytes 4194304 | tf_op jit(solution)/shard_map/all_to_all | solution.py:249
  218.1 0.0 copy-done.5
  218.1 0.5 convert_rsqrt_fusion.scales_ref
  218.6 46.9 %all-to-all-done.1.x_ref = bf16[64,128,128]{2,1,0:T(8,128)(2,1)S(1)} async-done(((bf16[64,128,128]{2,1,0:T(8,128)(2,1)}), bf16[64,128,128]{2,1,0:T(8,128)(2,1)S(1)}, u32[]{:S(2)}, u32[]{:S(2)}) %all-to-all-start.1) | async-done | bytes 2097184 | tf_op jit(solution)/shard_map/all_to_all | solution.py:249
  265.5 0.0 copy-start.1
  265.5 1.3 copy-done.1
  266.9 15.8 %boxcar.1 = f32[7168,128]{1,0:T(8,128)} custom-call(s32[128]{0:T(128)} %widths_ref.1, f32[128]{0:T(128)} %convert_rsqrt_fusion.scales_ref, bf16[64,128,128]{2,1,0:T(8,128)(2,1)} %copy-done.1), custom_call_target="tpu_custom_call" | custom-call | tf_op jit(solution)/shard_map/boxcar/pallas_call | solution.py:208
  282.7 6.7 %copy.16 = f32[128,28,2,128]{0,3,1,2:T(8,128)} copy(f32[128,28,2,128]{3,2,1,0:T(2,128)} %bitcast.20) | data formatting | bytes 7340032 | tf_op jit(solution)/shard_map/reshape | solution.py:252
  289.4 6.6 %copy.17 = f32[128,2,3584]{2,1,0:T(2,128)} copy(f32[128,2,3584]{0,2,1:T(8,128)} %bitcast.21) | data formatting | bytes 7340032 | tf_op jit(solution)/shard_map/reshape | solution.py:253
  (4 shorter events, 0.0 us)
Async XLA Ops:
  0.0 12.7 %copy-start.2 = (s32[512,128]{1,0:T(8,128)S(1)}, s32[512,128]{1,0:T(8,128)}, u32[]{:S(2)}) copy-start(s32[512,128]{1,0:T(8,128)} %param.7) | copy-start | bytes 786436
  49.6 6.7 %copy-start.6 = (s32[128]{0:T(128)S(1)}, s32[128]{0:T(128)}, u32[]{:S(2)}) copy-start(s32[128]{0:T(128)} %param.10) | copy-start | bytes 1540
  49.6 6.7 %copy-start.3 = (s32[4,2,128]{2,1,0:T(2,128)S(1)}, s32[4,2,128]{2,1,0:T(2,128)}, u32[]{:S(2)}) copy-start(s32[4,2,128]{2,1,0:T(2,128)} %param.8) | copy-start | bytes 12292
  49.6 6.9 %copy-start.4 = (s32[4,128]{1,0:T(4,128)S(1)}, s32[4,128]{1,0:T(4,128)}, u32[]{:S(2)}) copy-start(s32[4,128]{1,0:T(4,128)} %param.9) | copy-start | bytes 6148
  49.6 87.6 %all-to-all-start = ((bf16[16,128,768]{2,1,0:T(8,128)(2,1)}), bf16[16,128,768]{2,1,0:T(8,128)(2,1)S(1)}, u32[]{:S(2)}, u32[]{:S(2)}) async-start(bf16[16,128,768]{2,1,0:T(8,128)(2,1)} %level0.1), calls=%async_computation | async-start | bytes 6291456 | tf_op jit(solution)/shard_map/all_to_all | solution.py:247
  137.3 1.7 copy-start
  138.9 79.2 %copy-start.5 = (s32[128]{0:T(128)S(1)}, s32[128]{0:T(128)}, u32[]{:S(2)}) copy-start(s32[128]{0:T(128)} %widths_ref.1) | copy-start | bytes 1540
  213.0 52.5 %all-to-all-start.1 = ((bf16[64,128,128]{2,1,0:T(8,128)(2,1)}), bf16[64,128,128]{2,1,0:T(8,128)(2,1)S(1)}, u32[]{:S(2)}, u32[]{:S(2)}) async-start(bf16[64,128,128]{2,1,0:T(8,128)(2,1)} %tree.1), calls=%async_computation.1 | async-start | bytes 4194304 | tf_op jit(solution)/shard_map/all_to_all | solution.py:249
  265.5 1.3 copy-start.1

commit v2 on v1

v2 whole, which is shorter than its diff:
```python
import functools
import math

import jax
import jax.numpy as jnp
from jax import lax
from jax.experimental import pallas as pl
from jax.experimental.pallas import tpu as pltpu
from jax.sharding import PartitionSpec as P

MARGIN = 512
DL = 16
DM = 64
LANES = 128
SUBLANES = 8
GROUP = 16
UNROLL = 64
SPLITS = 2
half_root = 0.7071067811865476
f32 = jnp.float32
bf16 = jnp.bfloat16
VMEM_BYTES = 58 * 2**20


def level0_kernel(span, chunks, chunk, halo, delay_ref, x_ref, next_ref, out_ref, sel_ref):
    slab = pl.program_id(0)
    piece = pl.program_id(1)
    rows = delay_ref.shape[0]
    channels = delay_ref.shape[1]

    @pl.when((slab == 0) & (piece == 0))
    def _():
        for d in range(DL):
            sel_ref[d * rows : (d + 1) * rows, :] = jnp.where(
                delay_ref[...] == d, 1.0, 0.0
            ).astype(bf16)

    alive = jnp.where((piece + 1) * span < chunks, 1.0, 0.0).astype(bf16)
    x = jnp.concatenate([x_ref[0], next_ref[0] * alive], axis=1)
    total = jnp.zeros((rows, chunk * span), f32)
    per = 4
    for first in range(0, DL, per):
        y = jnp.dot(
            sel_ref[first * rows : (first + per) * rows, :], x, preferred_element_type=f32
        )
        for d in range(first, first + per):
            part = y[(d - first) * rows : (d - first + 1) * rows, :]
            total = total + part[:, d : d + chunk * span]
    value = (total * (1.0 / math.sqrt(channels))).astype(bf16)
    reach = -(-halo // chunk)
    for k in range(span):
        own = value[None, :, k * chunk : (k + 1) * chunk]
        index = piece * span + k
        here = slab * chunks + index
        out_ref[pl.ds(here, 1), :, 0:chunk] = own
        for back in range(1, reach + 1):
            stop = min((back + 1) * chunk, chunk + halo)
            width = stop - back * chunk

            @pl.when(index >= back)
            def _():
                out_ref[pl.ds(here - back, 1), :, back * chunk : stop] = own[:, :, :width]

            @pl.when(index + back >= chunks)
            def _():
                out_ref[pl.ds(here, 1), :, back * chunk : stop] = jnp.zeros((1, rows, width), bf16)


def level0(samples, channel_delay, parts, halo):
    slabs, channels, length = samples.shape
    rows = channel_delay.shape[1]
    chunks = parts // slabs
    chunk = length // chunks
    span = 2 if chunks % 2 == 0 else 1
    tiles = span * chunk // LANES
    last = length // LANES - 1
    return pl.pallas_call(
        functools.partial(level0_kernel, span, chunks, chunk, halo),
        grid=(slabs, chunks // span),
        in_specs=[
            pl.BlockSpec((rows, channels), lambda s, c: (0, 0)),
            pl.BlockSpec((1, channels, chunk * span), lambda s, c: (s, 0, c)),
            pl.BlockSpec(
                (1, channels, LANES), lambda s, c: (s, 0, jnp.minimum((c + 1) * tiles, last))
            ),
        ],
        out_specs=pl.BlockSpec((parts, rows, chunk + halo), lambda s, c: (0, 0, 0)),
        out_shape=jax.ShapeDtypeStruct((parts, rows, chunk + halo), bf16),
        scratch_shapes=[pltpu.VMEM((DL * rows, channels), bf16)],
        compiler_params=pltpu.CompilerParams(vmem_limit_bytes=VMEM_BYTES),
        name="level0",
    )(channel_delay.T, samples, samples)


def tree_kernel(levels, keep, low_ref, high_ref, amount_ref, dest_ref, *refs):
    x_refs, (out_ref, a_ref, b_ref, o_ref) = refs[:-4], refs[-4:]
    extent = x_refs[0].shape[1]
    rows = out_ref.shape[1]
    trials = low_ref.shape[1]
    cut = rows // len(x_refs)

    def stage(k, carry):
        for half, x_ref in enumerate(x_refs):
            for g in range(0, cut, GROUP):
                x = x_ref[pl.ds(pl.multiple_of(k * cut, GROUP) + g, GROUP), :].astype(f32)
                first = (k * rows + half * cut + g) * SUBLANES
                for j in range(SUBLANES):
                    if j * LANES < extent:
                        piece = x[:, j * LANES : (j + 1) * LANES]
                    else:
                        piece = jnp.zeros((GROUP, LANES), f32)
                    a_ref[pl.ds(first + j, GROUP, stride=SUBLANES), :] = piece
        return carry

    lax.fori_loop(0, trials // rows, stage, 0)
    lane = lax.broadcasted_iota(jnp.int32, (SUBLANES, LANES), 1)
    for level in range(levels):
        src, dst = (a_ref, b_ref) if level % 2 == 0 else (b_ref, a_ref)

        def merge(g, carry):
            for i in range(UNROLL):
                q = g * UNROLL + i
                low = pl.multiple_of(low_ref[level, q], SUBLANES)
                high = pl.multiple_of(high_ref[level, q], SUBLANES)
                amount = amount_ref[level, q]
                v_low = src[pl.ds(low, SUBLANES), :]
                v_high = src[pl.ds(high, SUBLANES), :]
                turned = pltpu.roll(v_high, amount, 1)
                after = pltpu.roll(turned, SUBLANES - 1, 0)
                moved = jnp.where(lane < amount, turned, after)
                value = ((v_low + moved) * half_root).astype(bf16).astype(f32)
                if level + 1 < levels:
                    dst[pl.ds(pl.multiple_of(q * SUBLANES, SUBLANES), SUBLANES), :] = value
                else:
                    o_ref[pl.ds(dest_ref[q], keep, stride=rows), :] = value[:keep]
            return carry

        lax.fori_loop(0, trials // UNROLL, merge, 0)

    def pack(g, carry):
        out_ref[g] = o_ref[pl.ds(pl.multiple_of(g * rows, rows), rows), :].astype(bf16)
        return carry

    lax.fori_loop(0, out_ref.shape[0], pack, 0)


def tree(low, high, amount, places, arrived, keep, rows):
    levels = low.shape[0]
    trials = low.shape[1]
    blocks = trials // rows * keep
    whole = pl.BlockSpec(memory_space=pltpu.VMEM)
    scalars = pl.BlockSpec(memory_space=pltpu.SMEM)
    return pl.pallas_call(
        functools.partial(tree_kernel, levels, keep),
        in_specs=[scalars] * 4 + [whole] * len(arrived),
        out_specs=whole,
        out_shape=jax.ShapeDtypeStruct((blocks, rows, LANES), bf16),
        scratch_shapes=[
            pltpu.VMEM((trials * SUBLANES, LANES), f32),
            pltpu.VMEM((trials * SUBLANES, LANES), f32),
            pltpu.VMEM((blocks * rows, LANES), f32),
        ],
        compiler_params=pltpu.CompilerParams(vmem_limit_bytes=VMEM_BYTES),
        name="tree",
    )(low, high, amount, places, *arrived)


def boxcar_kernel(valid, pitch, widths_ref, scales_ref, x_ref, out_ref, p_ref, t_ref):
    blocks, rows, _ = x_ref.shape
    slabs = out_ref.shape[1]
    per_slab = blocks // slabs
    row = lax.broadcasted_iota(jnp.int32, (LANES, 2 * LANES), 0)
    col = lax.broadcasted_iota(jnp.int32, (LANES, 2 * LANES), 1)
    sums = jnp.where(row < col, 1.0, 0.0).astype(bf16)

    for i in range(valid + 1):
        for s in range(slabs):
            y = jnp.dot(x_ref[s * per_slab + i], sums, preferred_element_type=f32)
            p_ref[pl.ds(i * slabs + s, rows, stride=pitch), :] = y[:, :LANES]
            t_ref[pl.ds(i * slabs + s, rows, stride=pitch), :] = y[:, LANES:]
    lane = lax.broadcasted_iota(jnp.int32, (SUBLANES, LANES), 1)

    def window(g, carry):
        for i in range(4):
            p = g * 4 + i
            scale = scales_ref[p]
            amount = LANES - widths_ref[p]
            base = pl.multiple_of(p * pitch, SUBLANES)
            for b in range(0, valid * slabs, SUBLANES):
                here = p_ref[pl.ds(base + b, SUBLANES), :]
                after = p_ref[pl.ds(base + b + slabs, SUBLANES), :]
                whole = t_ref[pl.ds(base + b, SUBLANES), :]
                end = jnp.where(
                    lane < amount,
                    pltpu.roll(here, amount, 1),
                    pltpu.roll(after, amount, 1) + whole,
                )
                value = (end - here) * scale
                for j in range(0, min(SUBLANES, valid * slabs - b), slabs):
                    t = (b + j) // slabs
                    out_ref[p, :, t * LANES : (t + 1) * LANES] = value[j : j + slabs]
        return carry

    lax.fori_loop(0, rows // 4, window, 0)


def boxcar(widths, arrived, slabs, valid):
    rows = arrived.shape[1]
    pitch = -(-(valid + 1) * slabs // SUBLANES) * SUBLANES + SUBLANES
    whole = pl.BlockSpec(memory_space=pltpu.VMEM)
    scalars = pl.BlockSpec(memory_space=pltpu.SMEM)
    return pl.pallas_call(
        functools.partial(boxcar_kernel, valid, pitch),
        in_specs=[scalars, scalars, whole],
        out_specs=whole,
        out_shape=jax.ShapeDtypeStruct((rows, slabs, valid * LANES), f32),
        scratch_shapes=[
            pltpu.VMEM((rows * pitch, LANES), f32),
            pltpu.VMEM((rows * pitch, LANES), f32),
        ],
        compiler_params=pltpu.CompilerParams(vmem_limit_bytes=VMEM_BYTES),
        name="boxcar",
    )(widths, 1.0 / jnp.sqrt(widths.astype(f32)), arrived)


def body(samples, channel_delay, merge_rows, merge_shift, destination, widths):
    slabs, length = samples.shape[1], samples.shape[2]
    rows = channel_delay.shape[1]
    parts = lax.axis_size("band")
    levels = merge_shift.shape[0]
    position = lax.axis_index("band")
    chunk = slabs * length // parts
    keep = chunk // LANES
    halo = -(-levels * (DM - 1) // LANES) * LANES

    bits = (2 ** jnp.arange(levels, dtype=jnp.int32))[:, None]
    low = (position & ~bits) * rows + merge_rows[:, 0]
    high = (position | bits) * rows + merge_rows[:, 1]
    owner, slot = destination // rows, destination % rows
    place = owner * (keep * rows) + slot
    tables = jnp.concatenate([low, high, merge_shift, place[None]], axis=0)
    by_slab = jnp.transpose(samples, (1, 0, 2))
    arrived = []
    cut = rows // SPLITS
    for i in range(SPLITS):
        outgoing = level0(by_slab, channel_delay[:, i * cut : (i + 1) * cut], parts, halo)
        block = lax.all_to_all(outgoing, "band", split_axis=0, concat_axis=0, tiled=True)
        arrived.append(block.reshape(parts * cut, chunk + halo))
        if i == 0:
            arrived[0], tables = lax.optimization_barrier((arrived[0], tables))
    tables = lax.all_gather(tables, "band", axis=1, tiled=True)
    low = tables[:levels] * SUBLANES
    high = tables[levels : 2 * levels] * SUBLANES
    amount = LANES - tables[2 * levels : 3 * levels]
    places = tables[3 * levels]
    merged = tree(low, high, amount, places, arrived, keep, rows)
    grouped = lax.all_to_all(merged, "band", split_axis=0, concat_axis=0, tiled=True)
    valid = (length - MARGIN) // LANES
    return boxcar(widths, grouped, slabs, valid)


def solution(mesh):
    return jax.shard_map(
        body,
        mesh=mesh,
        in_specs=(
            P(("group", "band"), None, None),
            P("band", None),
            P(None, None, "band"),
            P(None, "band"),
            P("band"),
            P("band"),
        ),
        out_specs=P(("group", "band"), None, None),
        check_vma=False,
    )
```

time: 297 us -> 235 us (0.79)
  Pallas kernels: 126 us -> 86.6 us
  blocking collectives: 79.5 us -> 45.8 us
  waiting for transfers between devices: 46.9 us -> 65.7 us
  local copies, waits for them, and re-layouts: 30.5 us -> 18.5 us
  starting transfers between devices: 11.8 us -> 16.6 us
    all_gather x1, blocking collectives: 79.5 us -> 45.8 us  [body(): tables = lax.all_gather(tables, 'band', axis=1, tiled=True)]
    pallas_call x1, Pallas kernels: 74.1 us -> 44 us  [tree(): pl.pallas_call(functools.partial(tree_kernel, levels, keep), in_specs=[sc...]
    all_to_all x1 -> x2, waiting for transfers between devices: 0.01 us -> 18.8 us  [body(): lax.all_to_all(outgoing, 'band', split_axis=0, concat_axis=0, tiled=True)]
    reshape x2 -> x0, local copies, waits for them, and re-layouts: 13.3 us -> none  [the longest x1 6.71 us: body(): result = result.reshape(rows, valid, slabs, LANES).transpose(0, 2, 1, 3)]
    pallas_call x2 -> x3, Pallas kernels: 51.9 us -> 42.6 us  [the longest x2 33.1 us: level0(): pl.pallas_call(functools.partial(level0_kernel, span, chunks, chunk, halo...]
    all_to_all x1 -> x2, starting transfers between devices: 6.7 us -> 11.5 us  [body(): lax.all_to_all(outgoing, 'band', split_axis=0, concat_axis=0, tiled=True)]
    unnamed x16 -> x17, local copies, waits for them, and re-layouts: 16.6 us -> 16.7 us
  transfers between devices with their start and end apart: 2 -> 3, of which waited for: 1 -> 2; matrix products, arithmetic and copies ran while one was open for 1% -> 1% of each run, Pallas kernels for 0% -> 7%
where the time goes in v2:
time: 235 us
  Pallas kernels  86.6 us (37%)
  waiting for transfers between devices  65.7 us (28%)
  blocking collectives  45.8 us (19%)
  local copies, waits for them, and re-layouts  18.5 us (8%)
  starting transfers between devices  16.6 us (7%)
    all_to_all x1, waiting for transfers between devices, body(): lax.all_to_all(merged, 'band', split_axis=0, concat_axis=0, tiled=True)  46.9 us
    all_gather x1, blocking collectives, body(): tables = lax.all_gather(tables, 'band', axis=1, tiled=True)  45.8 us
    pallas_call x1, Pallas kernels, tree(): pl.pallas_call(functools.partial(tree_kernel, levels, keep), in_specs=[sc...  44 us
    pallas_call x2, Pallas kernels, level0(): pl.pallas_call(functools.partial(level0_kernel, span, chunks, chunk, halo...  33.1 us
    all_to_all x2, waiting for transfers between devices, body(): lax.all_to_all(outgoing, 'band', split_axis=0, concat_axis=0, tiled=True)  18.8 us
    unnamed x17, local copies, waits for them, and re-layouts  16.7 us
    all_to_all x2, starting transfers between devices, body(): lax.all_to_all(outgoing, 'band', split_axis=0, concat_axis=0, tiled=True)  11.5 us
    pallas_call x1, Pallas kernels, boxcar(): pl.pallas_call(functools.partial(boxcar_kernel, valid, pitch), in_specs=[...  9.52 us
  transfers between devices with their start and end apart: 3, of which 2 were waited for; matrix products, arithmetic and copies ran while one was open for 1% of the time, Pallas kernels for 7%

profile of v2, /device:TPU:13, one launch (start us, length us, event | category | flops | bytes accessed | tf_op | source)
XLA Modules:
  0.0 234.6 jit_solution(13386944846776552527)
XLA Ops:
  0.0 1.2 fusion.4
  1.2 0.8 copy.12
  2.0 12.7 %copy.17 = bf16[512,2,4096]{2,0,1:T(8,128)(2,1)} copy(bf16[512,2,4096]{2,1,0:T(2,128)(2,1)} %param.6) | data formatting | bytes 16777216 | tf_op args[0]
  14.6 16.5 %level0.2 = bf16[16,64,768]{2,1,0:T(8,128)(2,1)} custom-call(s32[64,512]{1,0:T(8,128)} %bitcast.22, bf16[2,512,4096]{2,1,0:T(8,128)(2,1)} %bitcast.16, bf16[2,512,4096]{2,1,0:T(8,128)(2,1)} %bitcast.17), custom_call_target="tpu_custom_call" | custom-call | tf_op jit(solution)/shard_map/level0/pallas_call | solution.py:77
  31.1 6.6 %all-to-all-start = ((bf16[16,64,768]{2,1,0:T(8,128)(2,1)}), bf16[16,64,768]{2,1,0:T(8,128)(2,1)S(1)}, u32[]{:S(2)}, u32[]{:S(2)}) async-start(bf16[16,64,768]{2,1,0:T(8,128)(2,1)} %level0.2), calls=%async_computation | async-start | bytes 3145728 | tf_op jit(solution)/shard_map/all_to_all | solution.py:247
  37.7 0.8 copy.15
  38.5 16.6 %level0.3 = bf16[16,64,768]{2,1,0:T(8,128)(2,1)} custom-call(s32[64,512]{1,0:T(8,128)} %bitcast.23, bf16[2,512,4096]{2,1,0:T(8,128)(2,1)} %bitcast.18, bf16[2,512,4096]{2,1,0:T(8,128)(2,1)} %bitcast.19), custom_call_target="tpu_custom_call" | custom-call | tf_op jit(solution)/shard_map/level0/pallas_call | solution.py:77
  55.0 0.0 copy-start.6
  55.0 0.0 copy-start.3
  55.0 0.0 copy-start.4
  55.0 18.8 %all-to-all-done = bf16[16,64,768]{2,1,0:T(8,128)(2,1)S(1)} async-done(((bf16[16,64,768]{2,1,0:T(8,128)(2,1)}), bf16[16,64,768]{2,1,0:T(8,128)(2,1)S(1)}, u32[]{:S(2)}, u32[]{:S(2)}) %all-to-all-start) | async-done | bytes 1572896 | tf_op jit(solution)/shard_map/all_to_all | solution.py:247
  73.9 0.0 copy-start.1
  73.9 4.9 %all-to-all-start.1 = ((bf16[16,64,768]{2,1,0:T(8,128)(2,1)}), bf16[16,64,768]{2,1,0:T(8,128)(2,1)S(1)}, u32[]{:S(2)}, u32[]{:S(2)}) async-start(bf16[16,64,768]{2,1,0:T(8,128)(2,1)} %level0.3), calls=%async_computation.1 | async-start | bytes 3145728 | tf_op jit(solution)/shard_map/all_to_all | solution.py:247
  78.8 0.0 copy-done.6
  78.8 0.0 copy-done.3
  78.8 0.1 broadcast_add_fusion.1
  78.9 0.1 broadcast_add_fusion
  79.0 0.0 copy-done.4
  79.0 45.8 %all_gather.3 = s32[13,2048]{1,0:T(8,128)S(1)} all-gather(s32[13,128]{1,0:T(8,128)S(1)} %pad_add_fusion), channel_id=1, replica_groups=mesh['group'=2,'band'=16] {'band'}, dimensions={1}, use_global_device_ids=true | all-gather | bytes 113152 | tf_op jit(solution)/shard_map/all_gather | solution.py:251
  124.8 0.6 slice.35
  125.4 0.7 slice_subtract_fusion
  126.1 0.0 all-to-all-done.1
  126.1 0.0 copy-start.2
  126.1 0.0 copy-done.1
  126.1 1.1 copy-done.2
  127.2 44.0 %tree.1 = bf16[64,128,128]{2,1,0:T(8,128)(2,1)} custom-call(s32[4,2048]{1,0:T(4,128)} %get-tuple-element.13.low_ref, s32[4,2048]{1,0:T(4,128)} %get-tuple-element.12.high_ref, s32[4,2048]{1,0:T(4,128)} %get-tuple-element.11.amount_ref, s32[2048]{0:T(1024)} %bitcast.24, bf16[1024,768]{1,0:T(8,128)(2,1)} %bitcast.20, bf16[1024,768]{1,0:T(8,128)(2,1)} %bitcast.21), custom_call_target="tpu_custom_call" | custom-call | tf_op jit(solution)/shard_map/tree/pallas_call | solution.py:153
  171.2 0.0 copy-start.5
  171.2 5.1 %all-to-all-start.2 = ((bf16[64,128,128]{2,1,0:T(8,128)(2,1)}), bf16[64,128,128]{2,1,0:T(8,128)(2,1)S(1)}, u32[]{:S(2)}, u32[]{:S(2)}) async-start(bf16[64,128,128]{2,1,0:T(8,128)(2,1)} %tree.1), calls=%async_computation.2 | async-start | bytes 4194304 | tf_op jit(solution)/shard_map/all_to_all | solution.py:257
  176.3 0.0 copy-done.5
  176.4 0.5 convert_rsqrt_fusion.scales_ref
  176.9 46.9 %all-to-all-done.2.x_ref = bf16[64,128,128]{2,1,0:T(8,128)(2,1)S(1)} async-done(((bf16[64,128,128]{2,1,0:T(8,128)(2,1)}), bf16[64,128,128]{2,1,0:T(8,128)(2,1)S(1)}, u32[]{:S(2)}, u32[]{:S(2)}) %all-to-all-start.2) | async-done | bytes 2097184 | tf_op jit(solution)/shard_map/all_to_all | solution.py:257
  223.8 0.0 copy-start
  223.8 1.3 copy-done
  225.1 9.5 %boxcar.1 = f32[128,2,3584]{2,1,0:T(2,128)} custom-call(s32[128]{0:T(128)} %widths_ref.1, f32[128]{0:T(128)} %convert_rsqrt_fusion.scales_ref, bf16[64,128,128]{2,1,0:T(8,128)(2,1)} %copy-done), custom_call_target="tpu_custom_call" | custom-call | tf_op jit(solution)/shard_map/boxcar/pallas_call | solution.py:212
  (4 shorter events, 0.0 us)
Async XLA Ops:
  31.1 42.7 %all-to-all-start = ((bf16[16,64,768]{2,1,0:T(8,128)(2,1)}), bf16[16,64,768]{2,1,0:T(8,128)(2,1)S(1)}, u32[]{:S(2)}, u32[]{:S(2)}) async-start(bf16[16,64,768]{2,1,0:T(8,128)(2,1)} %level0.2), calls=%async_computation | async-start | bytes 3145728 | tf_op jit(solution)/shard_map/all_to_all | solution.py:247
  55.0 23.8 %copy-start.6 = (s32[128]{0:T(128)S(1)}, s32[128]{0:T(128)}, u32[]{:S(2)}) copy-start(s32[128]{0:T(128)} %param.10) | copy-start | bytes 1540
  55.0 23.8 %copy-start.3 = (s32[4,2,128]{2,1,0:T(2,128)S(1)}, s32[4,2,128]{2,1,0:T(2,128)}, u32[]{:S(2)}) copy-start(s32[4,2,128]{2,1,0:T(2,128)} %param.8) | copy-start | bytes 12292
  55.0 24.0 %copy-start.4 = (s32[4,128]{1,0:T(4,128)S(1)}, s32[4,128]{1,0:T(4,128)}, u32[]{:S(2)}) copy-start(s32[4,128]{1,0:T(4,128)} %param.9) | copy-start | bytes 6148
  73.9 52.2 %copy-start.1 = (bf16[16,64,768]{2,1,0:T(8,128)(2,1)}, bf16[16,64,768]{2,1,0:T(8,128)(2,1)S(1)}, u32[]{:S(2)}) copy-start(bf16[16,64,768]{2,1,0:T(8,128)(2,1)S(1)} %all-to-all-done) | copy-start | bytes 4718596
  73.9 52.2 %all-to-all-start.1 = ((bf16[16,64,768]{2,1,0:T(8,128)(2,1)}), bf16[16,64,768]{2,1,0:T(8,128)(2,1)S(1)}, u32[]{:S(2)}, u32[]{:S(2)}) async-start(bf16[16,64,768]{2,1,0:T(8,128)(2,1)} %level0.3), calls=%async_computation.1 | async-start | bytes 3145728 | tf_op jit(solution)/shard_map/all_to_all | solution.py:247
  126.1 1.1 copy-start.2
  171.2 5.1 %copy-start.5 = (s32[128]{0:T(128)S(1)}, s32[128]{0:T(128)}, u32[]{:S(2)}) copy-start(s32[128]{0:T(128)} %widths_ref.1) | copy-start | bytes 1540
  171.2 52.5 %all-to-all-start.2 = ((bf16[64,128,128]{2,1,0:T(8,128)(2,1)}), bf16[64,128,128]{2,1,0:T(8,128)(2,1)S(1)}, u32[]{:S(2)}, u32[]{:S(2)}) async-start(bf16[64,128,128]{2,1,0:T(8,128)(2,1)} %tree.1), calls=%async_computation.2 | async-start | bytes 4194304 | tf_op jit(solution)/shard_map/all_to_all | solution.py:257
  223.8 1.3 copy-start

commit v3 on v2

--- a/solution.py
+++ b/solution.py
@@ -14,8 +14,7 @@
 LANES = 128
 SUBLANES = 8
 GROUP = 16
-UNROLL = 64
-SPLITS = 2
+UNROLL = 128
 half_root = 0.7071067811865476
 f32 = jnp.float32
 bf16 = jnp.bfloat16
@@ -223,6 +222,58 @@
     )(widths, 1.0 / jnp.sqrt(widths.astype(f32)), arrived)
 
 
+def exchange_kernel(parts, count, *refs):
+    sources, targets = refs[:count], refs[count : 2 * count]
+    send_sem, recv_sem, own_sem = refs[2 * count :]
+    me = lax.axis_index("band")
+    barrier = pltpu.get_barrier_semaphore()
+    for k in range(1, parts):
+        pl.semaphore_signal(barrier, inc=1, device_id={"band": me ^ k})
+    own = [
+        pltpu.make_async_copy(sources[a].at[me], targets[a].at[me], own_sem.at[a])
+        for a in range(count)
+    ]
+    for copy in own:
+        copy.start()
+    pl.semaphore_wait(barrier, parts - 1)
+    copies = []
+    for k in range(1, parts):
+        for a in range(count):
+            copies.append(
+                pltpu.make_async_remote_copy(
+                    src_ref=sources[a].at[me ^ k],
+                    dst_ref=targets[a].at[me],
+                    send_sem=send_sem.at[a, k],
+                    recv_sem=recv_sem.at[a, k],
+                    device_id={"band": me ^ k},
+                )
+            )
+            copies[-1].start()
+    for copy in own:
+        copy.wait()
+    for copy in copies:
+        copy.wait()
+
+
+def exchange(arrays, collective_id):
+    parts = arrays[0].shape[0]
+    count = len(arrays)
+    anywhere = pl.BlockSpec(memory_space=pl.ANY)
+    return pl.pallas_call(
+        functools.partial(exchange_kernel, parts, count),
+        in_specs=[anywhere] * count,
+        out_specs=[anywhere] * count,
+        out_shape=[jax.ShapeDtypeStruct(a.shape, a.dtype) for a in arrays],
+        scratch_shapes=[
+            pltpu.SemaphoreType.DMA((count, parts)),
+            pltpu.SemaphoreType.DMA((count, parts)),
+            pltpu.SemaphoreType.DMA((count,)),
+        ],
+        compiler_params=pltpu.CompilerParams(collective_id=collective_id, has_side_effects=True),
+        name="exchange",
+    )(*arrays)
+
+
 def body(samples, channel_delay, merge_rows, merge_shift, destination, widths):
     slabs, length = samples.shape[1], samples.shape[2]
     rows = channel_delay.shape[1]
@@ -239,16 +290,12 @@
     owner, slot = destination // rows, destination % rows
     place = owner * (keep * rows) + slot
     tables = jnp.concatenate([low, high, merge_shift, place[None]], axis=0)
+    tables = jnp.broadcast_to(tables[None], (parts,) + tables.shape)
     by_slab = jnp.transpose(samples, (1, 0, 2))
-    arrived = []
-    cut = rows // SPLITS
-    for i in range(SPLITS):
-        outgoing = level0(by_slab, channel_delay[:, i * cut : (i + 1) * cut], parts, halo)
-        block = lax.all_to_all(outgoing, "band", split_axis=0, concat_axis=0, tiled=True)
-        arrived.append(block.reshape(parts * cut, chunk + halo))
-        if i == 0:
-            arrived[0], tables = lax.optimization_barrier((arrived[0], tables))
-    tables = lax.all_gather(tables, "band", axis=1, tiled=True)
+    outgoing = level0(by_slab, channel_delay, parts, halo)
+    block, tables = exchange([outgoing, tables], 0)
+    arrived = [block.reshape(parts * rows, chunk + halo)]
+    tables = jnp.transpose(tables, (1, 0, 2)).reshape(tables.shape[1], parts * rows)
     low = tables[:levels] * SUBLANES
     high = tables[levels : 2 * levels] * SUBLANES
     amount = LANES - tables[2 * levels : 3 * levels]

time: 235 us -> 231 us (0.983)
  Pallas kernels: 86.6 us -> 158 us
  blocking collectives: 45.8 us -> 0 us
  waiting for transfers between devices: 65.7 us -> 46.8 us
  starting transfers between devices: 16.6 us -> 5.1 us
    pallas_call x0 -> x1, Pallas kernels: none -> 75.7 us  [exchange(): pl.pallas_call(functools.partial(exchange_kernel, parts, count), in_specs...]
    all_gather x1 -> x0, blocking collectives: 45.8 us -> none  [body(): tables = lax.all_gather(tables, 'band', axis=1, tiled=True)]
    all_to_all x2 -> x0, waiting for transfers between devices: 18.8 us -> none  [body(): lax.all_to_all(outgoing, 'band', split_axis=0, concat_axis=0, tiled=True)]
    all_to_all x2 -> x0, starting transfers between devices: 11.5 us -> none  [body(): lax.all_to_all(outgoing, 'band', split_axis=0, concat_axis=0, tiled=True)]
    pallas_call x2 -> x1, Pallas kernels: 33.1 us -> 29.9 us  [level0(): pl.pallas_call(functools.partial(level0_kernel, span, chunks, chunk, halo...]
    unnamed x17 -> x12, local copies, waits for them, and re-layouts: 16.7 us -> 15.9 us
  transfers between devices with their start and end apart: 3 -> 1, of which waited for: 2 -> 1; matrix products, arithmetic and copies ran while one was open for 1% -> 0% of each run, Pallas kernels for 7% -> 0%
where the time goes in v3:
time: 231 us; the launch traced here: 230 us
  Pallas kernels  158 us (68%)
  waiting for transfers between devices  46.8 us (20%)
  local copies, waits for them, and re-layouts  18 us (8%)
  starting transfers between devices  5.1 us (2%)
  other arithmetic  2.34 us (1%)
    pallas_call x1, Pallas kernels, exchange(): pl.pallas_call(functools.partial(exchange_kernel, parts, count), in_specs...  75.7 us
    all_to_all x1, waiting for transfers between devices, body(): lax.all_to_all(merged, 'band', split_axis=0, concat_axis=0, tiled=True)  46.8 us
    pallas_call x1, Pallas kernels, tree(): pl.pallas_call(functools.partial(tree_kernel, levels, keep), in_specs=[sc...  43 us
    pallas_call x1, Pallas kernels, level0(): pl.pallas_call(functools.partial(level0_kernel, span, chunks, chunk, halo...  29.9 us
    unnamed x12, local copies, waits for them, and re-layouts  15.9 us
    pallas_call x1, Pallas kernels, boxcar(): pl.pallas_call(functools.partial(boxcar_kernel, valid, pitch), in_specs=[...  9.52 us
    all_to_all x1, starting transfers between devices, body(): lax.all_to_all(merged, 'band', split_axis=0, concat_axis=0, tiled=True)  5.1 us
  transfers between devices with their start and end apart: 1, of which 1 were waited for; matrix products, arithmetic and copies ran while one was open for 0% of the time, Pallas kernels for 0%

profile of v3, /device:TPU:13, one launch (start us, length us, event | category | flops | bytes accessed | tf_op | source)
XLA Modules:
  0.0 230.4 jit_solution(17342365720293026018)
XLA Ops:
  0.0 1.8 copy.7
  1.8 0.0 copy-start.4
  1.8 0.0 copy-start.1
  1.8 12.7 %copy.14 = bf16[512,2,4096]{2,0,1:T(8,128)(2,1)} copy(bf16[512,2,4096]{2,1,0:T(2,128)(2,1)} %param.6) | data formatting | bytes 16777216 | tf_op args[0]
  14.5 0.0 copy-done.4
  14.5 0.0 copy-done.1
  14.6 0.0 copy-start.2
  14.6 29.9 %level0.1.refs_0_ = bf16[16,128,768]{2,1,0:T(8,128)(2,1)} custom-call(s32[128,512]{1,0:T(8,128)} %bitcast.24, bf16[2,512,4096]{2,1,0:T(8,128)(2,1)} %bitcast.21, bf16[2,512,4096]{2,1,0:T(8,128)(2,1)} %bitcast.22), custom_call_target="tpu_custom_call" | custom-call | tf_op jit(solution)/shard_map/level0/pallas_call | solution.py:76
  44.5 0.1 broadcast_add_fusion
  44.6 0.1 broadcast_add_fusion.1
  44.6 0.0 copy-done.2
  44.7 0.7 broadcast_in_dim.9.refs_1_
  45.3 75.7 %exchange.1 = (bf16[16,128,768]{2,1,0:T(8,128)(2,1)}, s32[16,13,128]{2,1,0:T(8,128)}) custom-call(bf16[16,128,768]{2,1,0:T(8,128)(2,1)} %level0.1.refs_0_, s32[16,13,128]{2,1,0:T(8,128)} %broadcast_in_dim.9.refs_1_), custom_call_target="tpu_custom_call" | custom-call | tf_op jit(solution)/shard_map/exchange/pallas_call | solution.py:262
  121.0 1.6 fusion
  122.6 1.4 slice.31
  124.0 43.0 %tree.1 = bf16[64,128,128]{2,1,0:T(8,128)(2,1)} custom-call(s32[4,2048]{1,0:T(4,128)} %get-tuple-element.11.low_ref, s32[4,2048]{1,0:T(4,128)} %get-tuple-element.10.high_ref, s32[4,2048]{1,0:T(4,128)} %get-tuple-element.9.amount_ref, s32[2048]{0:T(1024)} %bitcast.27, bf16[2048,768]{1,0:T(8,128)(2,1)} %bitcast.23), custom_call_target="tpu_custom_call" | custom-call | tf_op jit(solution)/shard_map/tree/pallas_call | solution.py:152
  167.0 0.0 copy-start.3
  167.0 5.1 %all-to-all-start = ((bf16[64,128,128]{2,1,0:T(8,128)(2,1)}), bf16[64,128,128]{2,1,0:T(8,128)(2,1)S(1)}, u32[]{:S(2)}, u32[]{:S(2)}) async-start(bf16[64,128,128]{2,1,0:T(8,128)(2,1)} %tree.1), calls=%async_computation | async-start | bytes 4194304 | tf_op jit(solution)/shard_map/all_to_all | solution.py:304
  172.1 0.0 copy-done.3
  172.1 0.6 convert_rsqrt_fusion.scales_ref
  172.7 46.8 %all-to-all-done.x_ref = bf16[64,128,128]{2,1,0:T(8,128)(2,1)S(1)} async-done(((bf16[64,128,128]{2,1,0:T(8,128)(2,1)}), bf16[64,128,128]{2,1,0:T(8,128)(2,1)S(1)}, u32[]{:S(2)}, u32[]{:S(2)}) %all-to-all-start) | async-done | bytes 2097184 | tf_op jit(solution)/shard_map/all_to_all | solution.py:304
  219.5 0.0 copy-start
  219.5 1.3 copy-done
  220.9 9.5 %boxcar.1 = f32[128,2,3584]{2,1,0:T(2,128)} custom-call(s32[128]{0:T(128)} %widths_ref.1, f32[128]{0:T(128)} %convert_rsqrt_fusion.scales_ref, bf16[64,128,128]{2,1,0:T(8,128)(2,1)} %copy-done), custom_call_target="tpu_custom_call" | custom-call | tf_op jit(solution)/shard_map/boxcar/pallas_call | solution.py:211
  (4 shorter events, 0.0 us)
Async XLA Ops:
  1.8 12.7 %copy-start.4 = (s32[128]{0:T(128)S(1)}, s32[128]{0:T(128)}, u32[]{:S(2)}) copy-start(s32[128]{0:T(128)} %param.10) | copy-start | bytes 1540
  1.8 12.7 %copy-start.1 = (s32[4,2,128]{2,1,0:T(2,128)S(1)}, s32[4,2,128]{2,1,0:T(2,128)}, u32[]{:S(2)}) copy-start(s32[4,2,128]{2,1,0:T(2,128)} %param.8) | copy-start | bytes 12292
  14.6 30.1 %copy-start.2 = (s32[4,128]{1,0:T(4,128)S(1)}, s32[4,128]{1,0:T(4,128)}, u32[]{:S(2)}) copy-start(s32[4,128]{1,0:T(4,128)} %param.9) | copy-start | bytes 6148
  167.0 5.1 %copy-start.3 = (s32[128]{0:T(128)S(1)}, s32[128]{0:T(128)}, u32[]{:S(2)}) copy-start(s32[128]{0:T(128)} %widths_ref.1) | copy-start | bytes 1540
  167.0 52.5 %all-to-all-start = ((bf16[64,128,128]{2,1,0:T(8,128)(2,1)}), bf16[64,128,128]{2,1,0:T(8,128)(2,1)S(1)}, u32[]{:S(2)}, u32[]{:S(2)}) async-start(bf16[64,128,128]{2,1,0:T(8,128)(2,1)} %tree.1), calls=%async_computation | async-start | bytes 4194304 | tf_op jit(solution)/shard_map/all_to_all | solution.py:304
  219.5 1.3 copy-start
